TPU v7x, 32 devices: a whole 2x2x4 slice. The times are simulated.
32 devices in a mesh: head: 2 (over core), blk: 2 (over x), dp: 8 (over z, y).
Axes of the slice: x: 2, y: 2, z: 4, core: 2. Of those that a mesh axis runs over, the one named last changes fastest.
Arguments:
- layer_in: bfloat16 [32, 1024, 768], P('dp', 'blk', 'head'), may hold values from -6 to 6
- segments: int32 [32, 1024], P('dp'), may hold values from 0 to 6, as said below
- block_perm: int32 [12, 2], P('head'), may hold values from 0 to 1, as said below
- w_query: bfloat16 [768, 768], P(None, 'head'), may hold values from -0.21875 to 0.21875
- b_query: float32 [768], P('head'), may hold values from -3 to 3
- w_key: bfloat16 [768, 768], P(None, 'head'), may hold values from -0.21875 to 0.21875
- w_value: bfloat16 [768, 768], P(None, 'head'), may hold values from -0.21875 to 0.21875
- b_value: float32 [768], P('head'), may hold values from -3 to 3
- w_attn_out: bfloat16 [768, 768], P('head'), may hold values from -0.625 to 0.625
- b_attn_out: float32 [768], P('head'), may hold values from -3 to 3
- norm1_gain: float32 [768], P('head'), may hold values from 0.5 to 1.5
- norm1_bias: float32 [768], P('head'), may hold values from -3 to 3
- w_up: bfloat16 [768, 3072], P(None, 'head'), may hold values from -0.21875 to 0.21875
- b_up: float32 [3072], P('head'), may hold values from -3 to 3
- w_down: bfloat16 [3072, 768], P('head'), may hold values from -0.109375 to 0.109375
- b_down: float32 [768], P('head'), may hold values from -3 to 3
- norm2_gain: float32 [768], P('head'), may hold values from 0.5 to 1.5
- norm2_bias: float32 [768], P('head'), may hold values from -3 to 3
- grad_out: float32 [32, 1024, 768], P('dp', 'blk', 'head'), may hold values from -6 to 6
Outputs:
- layer_out: float32 [32, 1024, 768], P('dp', 'blk', 'head')
- grad_in: float32 [32, 1024, 768], P('dp', 'blk', 'head')
- grad_w_query: float32 [768, 768], P(None, 'head')
- grad_b_query: float32 [768], P('head')
- grad_w_key: float32 [768, 768], P(None, 'head')
- grad_w_value: float32 [768, 768], P(None, 'head')
- grad_b_value: float32 [768], P('head')
- grad_w_attn_out: float32 [768, 768], P('head')
- grad_b_attn_out: float32 [768], P('head')
- grad_norm1_gain: float32 [768], P('head')
- grad_norm1_bias: float32 [768], P('head')
- grad_w_up: float32 [768, 3072], P(None, 'head')
- grad_b_up: float32 [3072], P('head')
- grad_w_down: float32 [3072, 768], P('head')
- grad_b_down: float32 [768], P('head')
- grad_norm2_gain: float32 [768], P('head')
- grad_norm2_bias: float32 [768], P('head')
Inputs may be any that keep to these rules, and one draw needn't show every extreme that they name: `segments`: within each sequence the numbers start at 0 at the first position, never fall, and rise by one at six positions: three in 1 to 383 and three in 640 to 1023. `block_perm`: each row is a permutation of the block numbers; exactly 6 rows exchange the two blocks and the others keep them in place.
All inputs are finite; a program needn't handle non-finite values.
Results may differ from a plain program's by a relative error of at most 0.014.
Values may be sent and summed in bfloat16 or wider, within the bound.
A program may use at most 192 MiB of HBM per device.

v0:
```python
import jax
import jax.numpy as jnp
from jax import lax
from jax.sharding import PartitionSpec as P

EPSILON = 1e-05
NEGATIVE = -1e30
ROOT_HALF = 0.7071067811865476
DENSITY_SCALE = 0.3989422804014327


def from_partner(array, axis, distance):
    return lax.ppermute(array, axis, [(i, i ^ 1 << distance) for i in range(lax.axis_size(axis))])


def product(left, right):
    return jnp.dot(left, right, preferred_element_type=jnp.float32)


def weight_product(left, right):
    return lax.dot_general(
        left, right, (((0,), (0,)), ((), ())), preferred_element_type=jnp.float32
    )


def back_product(left, right):
    return lax.dot_general(
        left, right, (((1,), (1,)), ((), ())), preferred_element_type=jnp.float32
    )


def row_total(values):
    return lax.psum(values, "head")


def normalize(summed, gain, bias, model_width):
    mean = row_total((jnp.sum(summed, axis=-1),))[0] / model_width
    centered = summed - mean[..., None]
    variance = row_total((jnp.sum(centered * centered, axis=-1),))[0] / model_width
    inverse = lax.rsqrt(variance + EPSILON)[..., None]
    unit = centered * inverse
    return (unit * gain + bias, unit, inverse)


def norm_back(grad, unit, inverse, gain, model_width):
    scaled = grad * gain
    plain_sum, unit_sum = row_total((jnp.sum(scaled, axis=-1), jnp.sum(scaled * unit, axis=-1)))
    return (
        scaled - plain_sum[..., None] / model_width - unit * unit_sum[..., None] / model_width
    ) * inverse


def gelu_slope(values):
    return (
        0.5 * (1.0 + lax.erf(values * ROOT_HALF))
        + values * jnp.exp(-0.5 * values * values) * DENSITY_SCALE
    )


def usable_mask(query_seg, keys_seg):
    allowed = query_seg[None, :, None] == keys_seg[:, None, :]
    covered = jnp.any(allowed, axis=-1, keepdims=True)
    return jnp.logical_or(allowed, jnp.logical_not(covered))


def attend(packed):
    query_part, key_part, value_part, query_seg, keys_seg = packed
    usable = usable_mask(query_seg, keys_seg)
    scores = jnp.einsum("qhd,khd->hqk", query_part, key_part, preferred_element_type=jnp.float32)
    masked = jnp.where(usable, scores, NEGATIVE)
    row_max = jnp.max(masked, axis=-1, keepdims=True)
    shifted = jnp.exp(masked - row_max)
    row_sum = jnp.sum(shifted, axis=-1, keepdims=True)
    mixing = (shifted / row_sum).astype(jnp.bfloat16)
    context = jnp.einsum("hqk,khd->qhd", mixing, value_part, preferred_element_type=jnp.float32)
    return (context.astype(jnp.bfloat16), (row_max + jnp.log(row_sum))[..., 0])


def attend_back(packed):
    query_part, key_part, value_part, query_seg, keys_seg, grad_part, log_part = packed
    usable = usable_mask(query_seg, keys_seg)
    scores = jnp.einsum("qhd,khd->hqk", query_part, key_part, preferred_element_type=jnp.float32)
    masked = jnp.where(usable, scores, NEGATIVE)
    mixing = jnp.exp(masked - log_part[..., None])
    grad_mixing = jnp.einsum(
        "qhd,khd->hqk", grad_part, value_part, preferred_element_type=jnp.float32
    )
    inner_sum = jnp.sum(mixing * grad_mixing, axis=-1, keepdims=True)
    grad_scores = (mixing * (grad_mixing - inner_sum)).astype(jnp.bfloat16)
    grad_value = jnp.einsum(
        "hqk,qhd->khd", mixing.astype(jnp.bfloat16), grad_part, preferred_element_type=jnp.float32
    )
    grad_query = jnp.einsum(
        "hqk,khd->qhd", grad_scores, key_part, preferred_element_type=jnp.float32
    )
    grad_key = jnp.einsum(
        "hqk,qhd->khd", grad_scores, query_part, preferred_element_type=jnp.float32
    )
    return (
        grad_query.astype(jnp.bfloat16),
        grad_key.astype(jnp.bfloat16),
        grad_value.astype(jnp.bfloat16),
    )


def on_device(
    layer_in,
    segments,
    block_perm,
    w_query,
    b_query,
    w_key,
    w_value,
    b_value,
    w_attn_out,
    b_attn_out,
    norm1_gain,
    norm1_bias,
    w_up,
    b_up,
    w_down,
    b_down,
    norm2_gain,
    norm2_bias,
    grad_out,
):
    seq_count, block_len, half_width = layer_in.shape
    model_width = w_query.shape[0]
    local_heads = block_perm.shape[0]
    block_count = block_perm.shape[1]
    head_cols = w_query.shape[1]
    head_width = head_cols // local_heads
    row_count = seq_count * block_len
    score_scale = head_width ** (-0.5)
    my_block = lax.axis_index("blk")
    full_in = lax.all_gather(layer_in, "head", axis=2, tiled=True)
    flat_in = full_in.reshape(row_count, model_width)
    queries = ((product(flat_in, w_query) + b_query) * score_scale).astype(jnp.bfloat16)
    key_rows = product(flat_in, w_key).astype(jnp.bfloat16)
    value_rows = (product(flat_in, w_value) + b_value).astype(jnp.bfloat16)
    key_value = jnp.stack([key_rows, value_rows]).reshape(2, seq_count, block_len, head_cols)
    partner = from_partner(key_value, "blk", 0)
    block_ids = jnp.arange(block_count, dtype=jnp.int32)
    key_block = jnp.sum(jnp.where(block_ids[None, :] == my_block, block_perm, 0), axis=1)
    crossed = key_block != my_block
    crossed_cols = jnp.repeat(crossed, head_width)
    chosen = jnp.where(crossed_cols, partner, key_value)
    seg_blocks = segments.reshape(seq_count, block_count, block_len)
    own_seg = jnp.sum(jnp.where(block_ids[None, :, None] == my_block, seg_blocks, 0), axis=1)
    onehot = (key_block[:, None] == block_ids[None, :]).astype(jnp.int32)
    key_seg = jnp.sum(onehot[None, :, :, None] * seg_blocks[:, None, :, :], axis=2)
    head_shape = (seq_count, block_len, local_heads, head_width)
    query_heads = queries.reshape(head_shape)
    key_heads = chosen[0].reshape(head_shape)
    value_heads = chosen[1].reshape(head_shape)
    context, log_total = lax.map(attend, (query_heads, key_heads, value_heads, own_seg, key_seg))
    context_flat = context.reshape(row_count, head_cols)
    attn_part = product(context_flat, w_attn_out).reshape(seq_count, block_len, model_width)
    attended = lax.psum_scatter(attn_part, "head", scatter_dimension=2, tiled=True)
    summed_attn = layer_in.astype(jnp.float32) + attended + b_attn_out
    normed_attn, unit_attn, inverse_attn = normalize(
        summed_attn, norm1_gain, norm1_bias, model_width
    )
    full_normed = lax.all_gather(normed_attn.astype(jnp.bfloat16), "head", axis=2, tiled=True)
    full_normed = full_normed.reshape(row_count, model_width)
    up_proj = product(full_normed, w_up) + b_up
    activated = jax.nn.gelu(up_proj, approximate=False).astype(jnp.bfloat16)
    down_part = product(activated, w_down).reshape(seq_count, block_len, model_width)
    reduced_ffn = lax.psum_scatter(down_part, "head", scatter_dimension=2, tiled=True)
    summed_ffn = normed_attn + reduced_ffn + b_down
    layer_out, unit_ffn, inverse_ffn = normalize(summed_ffn, norm2_gain, norm2_bias, model_width)
    grad_norm2_gain = jnp.sum(grad_out * unit_ffn, axis=(0, 1))
    grad_norm2_bias = jnp.sum(grad_out, axis=(0, 1))
    grad_ffn = norm_back(grad_out, unit_ffn, inverse_ffn, norm2_gain, model_width)
    grad_b_down = jnp.sum(grad_ffn, axis=(0, 1))
    full_grad_ffn = lax.all_gather(grad_ffn.astype(jnp.bfloat16), "head", axis=2, tiled=True)
    full_grad_ffn = full_grad_ffn.reshape(row_count, model_width)
    grad_w_down = weight_product(activated, full_grad_ffn)
    grad_act = back_product(full_grad_ffn, w_down)
    grad_up = (grad_act * gelu_slope(up_proj)).astype(jnp.bfloat16)
    grad_b_up = jnp.sum(grad_up.astype(jnp.float32), axis=0)
    grad_w_up = weight_product(full_normed, grad_up)
    back_ffn = back_product(grad_up, w_up).reshape(seq_count, block_len, model_width)
    grad_mid = grad_ffn + lax.psum_scatter(back_ffn, "head", scatter_dimension=2, tiled=True)
    grad_norm1_gain = jnp.sum(grad_mid * unit_attn, axis=(0, 1))
    grad_norm1_bias = jnp.sum(grad_mid, axis=(0, 1))
    grad_attn = norm_back(grad_mid, unit_attn, inverse_attn, norm1_gain, model_width)
    grad_b_attn_out = jnp.sum(grad_attn, axis=(0, 1))
    full_grad_attn = lax.all_gather(grad_attn.astype(jnp.bfloat16), "head", axis=2, tiled=True)
    full_grad_attn = full_grad_attn.reshape(row_count, model_width)
    grad_w_attn_out = weight_product(context_flat, full_grad_attn)
    grad_context = back_product(full_grad_attn, w_attn_out).astype(jnp.bfloat16).reshape(head_shape)
    grad_queries, grad_keys, grad_values = lax.map(
        attend_back,
        (query_heads, key_heads, value_heads, own_seg, key_seg, grad_context, log_total),
    )
    grad_pair = jnp.stack([grad_keys, grad_values]).reshape(2, seq_count, block_len, head_cols)
    returned = from_partner(grad_pair, "blk", 0)
    own_pair = jnp.where(crossed_cols, returned, grad_pair).reshape(2, row_count, head_cols)
    grad_query_pre = (
        grad_queries.reshape(row_count, head_cols).astype(jnp.float32) * score_scale
    ).astype(jnp.bfloat16)
    grad_b_query = jnp.sum(grad_query_pre.astype(jnp.float32), axis=0)
    grad_w_query = weight_product(flat_in, grad_query_pre)
    grad_w_key = weight_product(flat_in, own_pair[0])
    grad_w_value = weight_product(flat_in, own_pair[1])
    grad_b_value = jnp.sum(own_pair[1].astype(jnp.float32), axis=0)
    back_input = (
        back_product(grad_query_pre, w_query)
        + back_product(own_pair[0], w_key)
        + back_product(own_pair[1], w_value)
    ).reshape(seq_count, block_len, model_width)
    grad_in = grad_attn + lax.psum_scatter(
        back_input.astype(jnp.bfloat16), "head", scatter_dimension=2, tiled=True
    ).astype(jnp.float32)
    (
        grad_w_query,
        grad_b_query,
        grad_w_key,
        grad_w_value,
        grad_b_value,
        grad_w_attn_out,
        grad_b_attn_out,
        grad_norm1_gain,
        grad_norm1_bias,
        grad_w_up,
        grad_b_up,
        grad_w_down,
        grad_b_down,
        grad_norm2_gain,
        grad_norm2_bias,
    ) = lax.psum(
        (
            grad_w_query,
            grad_b_query,
            grad_w_key,
            grad_w_value,
            grad_b_value,
            grad_w_attn_out,
            grad_b_attn_out,
            grad_norm1_gain,
            grad_norm1_bias,
            grad_w_up,
            grad_b_up,
            grad_w_down,
            grad_b_down,
            grad_norm2_gain,
            grad_norm2_bias,
        ),
        ("blk", "dp"),
    )
    return (
        layer_out,
        grad_in,
        grad_w_query,
        grad_b_query,
        grad_w_key,
        grad_w_value,
        grad_b_value,
        grad_w_attn_out,
        grad_b_attn_out,
        grad_norm1_gain,
        grad_norm1_bias,
        grad_w_up,
        grad_b_up,
        grad_w_down,
        grad_b_down,
        grad_norm2_gain,
        grad_norm2_bias,
    )


def solution(mesh):
    placed = (
        P("dp", "blk", "head"),
        P("dp", None),
        P("head", None),
        P(None, "head"),
        P("head"),
        P(None, "head"),
        P(None, "head"),
        P("head"),
        P("head", None),
        P("head"),
        P("head"),
        P("head"),
        P(None, "head"),
        P("head"),
        P("head", None),
        P("head"),
        P("head"),
        P("head"),
        P("dp", "blk", "head"),
    )
    return jax.shard_map(
        on_device,
        mesh=mesh,
        in_specs=placed,
        out_specs=(
            P("dp", "blk", "head"),
            P("dp", "blk", "head"),
            P(None, "head"),
            P("head"),
            P(None, "head"),
            P(None, "head"),
            P("head"),
            P("head", None),
            P("head"),
            P("head"),
            P("head"),
            P(None, "head"),
            P("head"),
            P("head", None),
            P("head"),
            P("head"),
            P("head"),
        ),
        check_vma=False,
    )
```

profile of v0, /device:TPU:0, one launch (start us, length us, event | category | flops | bytes accessed | tf_op | source)
XLA Modules:
  0.0 1006.5 jit_solution(473974311197727286)
XLA Ops:
  8.0 16.4 %all-gather.5.cloned.1.call-done = bf16[4,512,768]{2,1,0:T(8,128)(2,1)} async-done(((bf16[4,512,384]{2,1,0:T(8,128)(2,1)}), bf16[4,512,768]{2,1,0:T(8,128)(2,1)}) %all-gather.5.cloned.1.call-update) | async-done | bytes 3145744 | tf_op jit(solution)/shard_map/all_gather | solution.py:136
  49.3 53.7 %collective-permute-done = bf16[2,4,512,384]{3,2,1,0:T(8,128)(2,1)} collective-permute-done((bf16[2,4,512,384]{3,2,1,0:T(8,128)(2,1)}, bf16[2,4,512,384]{3,2,1,0:T(8,128)(2,1)}, u32[]{:S(2)}, u32[]{:S(2)}) %collective-permute-start) | collective-permute-done | bytes 3145760 | tf_op jit(solution)/shard_map/ppermute | solution.py:13
  113.9 42.4 %while.26 = (s32[]{:T(128)}, bf16[4,512,6,64]{1,3,2,0:T(8,128)(2,1)}, f32[4,6,512]{2,1,0:T(8,128)}, bf16[4,512,6,64]{1,3,2,0:T(8,128)(2,1)}, s32[4,512]{1,0:T(4,...) while((s32[]{:T(128)}, ...), condition=%wide.region_7.8_spmd, body=%wide.region_3.7_spmd.sunk | while | flops 429585408 | bytes 20656240 | solution.py:156
  156.3 5.9 fusion.69
  162.3 15.8 %reduce-scatter.7.cloned.1.call-done = f32[4,512,384]{2,1,0:T(8,128)} async-done(((f32[4,512,768]{2,1,0:T(8,128)}), f32[4,512,384]{2,1,0:T(8,128)}) %reduce-scatter.7.cloned.1.call-update) | async-done | bytes 3145744 | tf_op jit(solution)/shard_map/reduce_scatter | solution.py:159
  193.3 13.3 %all-gather.7.cloned.1.call-done = bf16[4,512,768]{2,1,0:T(8,128)(2,1)} async-done(((bf16[4,512,384]{2,1,0:T(8,128)(2,1)}), bf16[4,512,768]{2,1,0:T(8,128)(2,1)}) %all-gather.7.cloned.1.call-update) | async-done | bytes 3145744 | tf_op jit(solution)/shard_map/all_gather | solution.py:164
  206.6 33.6 %fusion.54 = (bf16[2048,1536]{1,0:T(8,128)(2,1)S(1)}, f32[2048,1536]{1,0:T(8,128)}) fusion(f32[1536]{0:T(1024)S(1)} %copy-done.51, bf16[2048,768]{1,0:T(8,128)(2,1)} %bitcast.233, bf16[768,1536]{1,0:T(8,128)(2,1)S(1)} %copy-done), kind=kOutput, calls=%fused_computation.67 | convolution fusion | flops 5039456256 | bytes 24385536 | tf_op jit(solution)/shard_map/dot_general | solution.py:17
  240.3 6.9 fusion.78
  247.2 15.8 %reduce-scatter.9.cloned.1.call-done = f32[4,512,384]{2,1,0:T(8,128)} async-done(((f32[4,512,768]{2,1,0:T(8,128)}), f32[4,512,384]{2,1,0:T(8,128)}) %reduce-scatter.9.cloned.1.call-update) | async-done | bytes 3145744 | tf_op jit(solution)/shard_map/reduce_scatter | solution.py:169
  282.7 6.5 fusion.72
  292.4 13.4 %all-gather.9.cloned.1.call-done = bf16[4,512,768]{2,1,0:T(8,128)(2,1)} async-done(((bf16[4,512,384]{2,1,0:T(8,128)(2,1)}), bf16[4,512,768]{2,1,0:T(8,128)(2,1)}) %all-gather.9.cloned.1.call-update) | async-done | bytes 3145744 | tf_op jit(solution)/shard_map/all_gather | solution.py:176
  305.8 12.6 %convert_reduce_fusion = (f32[1536]{0:T(1024)}, bf16[2048,1536]{1,0:T(8,128)(2,1)S(1)}) fusion(f32[2048,1536]{1,0:T(8,128)} %get-tuple-element.354, f32[1536]{0:T(1024)S(1)} %copy-done.51, bf16[2048,768]{1,0:T(8,128)(2,1)} %bitcast.235, bf16[1536,768]{1,0:T(8,128)(2,1)} %param.37), kind=kOutput, calls=%fused_computation.74 | convolution fusion | flops 4872731136 | bytes 24391680 | tf_op jit(solution)/shard_map/dot_general | solution.py:27
  318.4 6.9 fusion.79
  325.4 15.8 %reduce-scatter.11.cloned.1.call-done = f32[4,512,384]{2,1,0:T(8,128)} async-done(((f32[4,512,768]{2,1,0:T(8,128)}), f32[4,512,384]{2,1,0:T(8,128)}) %reduce-scatter.11.cloned.1.call-update) | async-done | bytes 3145744 | tf_op jit(solution)/shard_map/reduce_scatter | solution.py:184
  341.1 5.9 multiply_reduce_fusion.2
  357.5 13.4 %all-gather.11.cloned.1.call-done = bf16[4,512,768]{2,1,0:T(8,128)(2,1)} async-done(((bf16[4,512,384]{2,1,0:T(8,128)(2,1)}), bf16[4,512,768]{2,1,0:T(8,128)(2,1)}) %all-gather.11.cloned.1.call-update) | async-done | bytes 3145744 | tf_op jit(solution)/shard_map/all_gather | solution.py:189
  386.7 71.7 %while.27 = (s32[]{:T(128)}, bf16[4,512,6,64]{1,3,2,0:T(8,128)(2,1)}, bf16[4,512,6,64]{1,3,2,0:T(8,128)(2,1)}, bf16[4,512,6,64]{1,3,2,0:T(8,128)(2,1)}, bf16[4,5...) while((s32[]{:T(128)}, ...), condition=%wide.region_30.31_spmd, body=%wide.region_27.30_spmd.sunk | while | flops 1026094080 | bytes 51263624 | solution.py:193
  470.8 64.6 %collective-permute-done.1 = bf16[2,4,512,384]{3,2,1,0:T(8,128)(2,1)S(1)} collective-permute-done((bf16[2,4,512,384]{3,2,1,0:T(8,128)(2,1)S(1)}, bf16[2,4,512,384]{3,2,1,0:T(8,128)(2,1)S(1)}, u32[]{:S(2)}, u32[]{:S(2)}) %collective-permute-start.1) | collective-permute-done | bytes 3145760 | tf_op jit(solution)/shard_map/ppermute | solution.py:13
  543.0 6.2 copy.116
  557.0 9.3 fusion.84
  566.3 6.9 fusion.83
  584.8 81.6 %all-reduce = (f32[384]{0:T(512)}, f32[384]{0:T(512)}, f32[384]{0:T(512)}, f32[384]{0:T(512)}, f32[384]{0:T(512)}, /*index=5*/f32[1536]{0:T(1024)}, f32[384]{0:T(512)}, f32[384]{0:T(512)}, f32[384]{0:T(512)}) all-reduce(f32[384]{0:T(512)S(1)} %reduce_sum.212, ...), channel_id=1, replica_groups=mesh['head'=2,'blk'=2,'dp'=8] {'blk','dp'}, use_global_device_ids=true, to_apply=%region_34.35 | all-reduce | flops 4608 | bytes 36864 | tf_op jit(solution)/shard_map/psum | solution.py:232
  676.7 308.5 %all-reduce.6.cloned.1.call-done = (f32[768,384]{0,1:T(8,128)}, f32[768,384]{0,1:T(8,128)}, f32[768,384]{0,1:T(8,128)}, f32[384,768]{1,0:T(8,128)}, f32[768,1536]{1,0:T(8,128)}, /*index=5*/f32[1536,768]{1,0:T(8,128)}) async-done(((f32[768,384]{0,1:T(8,128)}, f32[768,384]{0,1:T(8,128)}, f32[768,384]{0,1:T(8,128)}, f32[384,768]{1,0:T(8,128)}, f32[768,1536]{1,0:T(8,128)}, /*index=5*/f32[1536,768]{1,0:T(8,128)}), ...) | async-done | bytes 14155792 | tf_op jit(solution)/shard_map/psum | solution.py:232
  991.8 5.5 copy.156
  (298 shorter events, 273.1 us)
Async XLA Ops:
  7.2 199.4 %copy-start = (bf16[768,1536]{1,0:T(8,128)(2,1)S(1)}, bf16[768,1536]{1,0:T(8,128)(2,1)}, u32[]{:S(2)}) copy-start(bf16[768,1536]{1,0:T(8,128)(2,1)} %param.35) | copy-start | bytes 7077892
  7.2 17.1 %all-gather.5.cloned.1.call-start = ((), (), s32[]{:S(2)}) async-start(), calls=%async_computation.4 | async-start | bytes 4718592 | tf_op jit(solution)/shard_map/all_gather | solution.py:136
  7.9 170.1 %reduce-scatter.7.cloned.1.call-start = ((), (), s32[]{:S(2)}) async-start(), calls=%async_computation.5 | async-start | bytes 9437184 | tf_op jit(solution)/shard_map/reduce_scatter | solution.py:159
  32.4 70.6 %collective-permute-start = (bf16[2,4,512,384]{3,2,1,0:T(8,128)(2,1)}, bf16[2,4,512,384]{3,2,1,0:T(8,128)(2,1)}, u32[]{:S(2)}, u32[]{:S(2)}) collective-permute-start(bf16[2,4,512,384]{3,2,1,0:T(8,128)(2,1)} %pad_maximum_fusion), channel_id=1, source_target_pairs={{0,8},{8,0},{1,9},{9,1},{2,10},{10,2},{3,11},{11,3},{4,12},{12,4},... | collective-permute-start | bytes 9437192 | tf_op jit(solution)/shard_map/ppermute | solution.py:13
  34.4 68.6 %copy-start.41 = (pred[384]{0:T(512)(128)(4,1)}, pred[384]{0:T(512)(128)(4,1)S(1)}, u32[]{:S(2)}) copy-start(pred[384]{0:T(512)(128)(4,1)S(1)} %reshape.188) | copy-start | bytes 1156
  46.2 56.7 %copy-start.13 = (bf16[2048,384]{1,0:T(8,128)(2,1)S(1)}, bf16[2048,384]{1,0:T(8,128)(2,1)}, u32[]{:S(2)}) copy-start(bf16[2048,384]{1,0:T(8,128)(2,1)} %copy-done.12) | copy-start | bytes 4718596
  46.2 56.8 %copy-start.15 = (bf16[2048,384]{1,0:T(8,128)(2,1)S(1)}, bf16[2048,384]{1,0:T(8,128)(2,1)}, u32[]{:S(2)}) copy-start(bf16[2048,384]{1,0:T(8,128)(2,1)} %copy-done.14) | copy-start | bytes 4718596
  113.9 42.4 %copy-start.23 = (bf16[384,768]{1,0:T(8,128)(2,1)S(1)}, bf16[384,768]{1,0:T(8,128)(2,1)}, u32[]{:S(2)}) copy-start(bf16[384,768]{1,0:T(8,128)(2,1)} %param.31) | copy-start | bytes 1769476
  162.2 15.9 %copy-start.39 = (f32[384]{0:T(512)S(1)}, f32[384]{0:T(512)}, u32[]{:S(2)}) copy-start(f32[384]{0:T(512)} %param.32) | copy-start | bytes 4612
  162.2 44.4 %all-gather.7.cloned.1.call-start = ((), (), s32[]{:S(2)}) async-start(), calls=%async_computation.6 | async-start | bytes 4718592 | tf_op jit(solution)/shard_map/all_gather | solution.py:164
  190.1 16.6 %copy-start.51 = (f32[1536]{0:T(1024)S(1)}, f32[1536]{0:T(1024)}, u32[]{:S(2)}) copy-start(f32[1536]{0:T(1024)} %param.36) | copy-start | bytes 18436
  193.2 69.8 %reduce-scatter.9.cloned.1.call-start = ((), (), s32[]{:S(2)}) async-start(), calls=%async_computation.7 | async-start | bytes 9437184 | tf_op jit(solution)/shard_map/reduce_scatter | solution.py:169
  206.6 33.7 %copy-start.50 = (bf16[1536,768]{1,0:T(8,128)(2,1)S(1)}, bf16[1536,768]{1,0:T(8,128)(2,1)}, u32[]{:S(2)}) copy-start(bf16[1536,768]{1,0:T(8,128)(2,1)} %param.37) | copy-start | bytes 7077892
  247.1 15.9 %copy-start.43 = (f32[384]{0:T(512)S(1)}, f32[384]{0:T(512)}, u32[]{:S(2)}) copy-start(f32[384]{0:T(512)} %param.38) | copy-start | bytes 4612
  247.2 58.6 %all-gather.9.cloned.1.call-start = ((), (), s32[]{:S(2)}) async-start(), calls=%async_computation.8 | async-start | bytes 4718592 | tf_op jit(solution)/shard_map/all_gather | solution.py:176
  292.3 48.8 %reduce-scatter.11.cloned.1.call-start = ((), (), s32[]{:S(2)}) async-start(), calls=%async_computation.9 | async-start | bytes 9437184 | tf_op jit(solution)/shard_map/reduce_scatter | solution.py:184
  325.3 45.6 %all-gather.11.cloned.1.call-start = ((), (), s32[]{:S(2)}) async-start(), calls=%async_computation.10 | async-start | bytes 4718592 | tf_op jit(solution)/shard_map/all_gather | solution.py:189
  356.1 14.8 %copy-start.24 = (bf16[384,768]{1,0:T(8,128)(2,1)S(1)}, bf16[384,768]{1,0:T(8,128)(2,1)}, u32[]{:S(2)}) copy-start(bf16[384,768]{1,0:T(8,128)(2,1)} %param.31) | copy-start | bytes 1769476
  357.5 308.9 %reduce-scatter.13.cloned.1.call-start = ((), (), s32[]{:S(2)}) async-start(), calls=%async_computation.11 | async-start | bytes 4718592
  465.0 70.4 %collective-permute-start.1 = (bf16[2,4,512,384]{3,2,1,0:T(8,128)(2,1)S(1)}, bf16[2,4,512,384]{3,2,1,0:T(8,128)(2,1)S(1)}, u32[]{:S(2)}, u32[]{:S(2)}) collective-permute-start(bf16[2,4,512,384]{3,2,1,0:T(8,128)(2,1)S(1)} %pad_maximum_fusion.1), channel_id=1, source_target_pairs={{0,8},{8,0},{1,9},{9,1},{2,10},{10,2},{3,11},{11,3},{4,12},{12,4},... | collective-permute-start | bytes 9437192 | tf_op jit(solution)/shard_map/ppermute | solution.py:13
  468.9 66.4 %copy-start.7 = (bf16[1,4,512,384]{3,2,1,0:T(8,128)(2,1)S(1)}, bf16[1,4,512,384]{3,2,1,0:T(8,128)(2,1)}, u32[]{:S(2)}) copy-start(bf16[1,4,512,384]{3,2,1,0:T(8,128)(2,1)} %copy.105) | copy-start | bytes 4718596
  468.9 66.4 %copy-start.42 = (pred[384]{0:T(512)(128)(4,1)S(1)}, pred[384]{0:T(512)(128)(4,1)}, u32[]{:S(2)}) copy-start(pred[384]{0:T(512)(128)(4,1)} %copy-done.41) | copy-start | bytes 1156
  553.7 431.5 %all-reduce.6.cloned.1.call-start = ((), (), s32[]{:S(2)}) async-start(), calls=%async_computation.12 | async-start | bytes 28311552 | tf_op jit(solution)/shard_map/psum | solution.py:232
  555.1 11.2 %slice-start.2 = ((s8[6291456]{0:T(1024)(128)(4,1)}), s8[4194304]{0:T(1024)(128)(4,1)S(1)}, s32[]{:S(2)}) async-start(s8[6291456]{0:T(1024)(128)(4,1)} %bitcast.239), calls=%async_computation.15 | async-start | bytes 8388608
  (47 other events, 194.8 us)
Sparse Core Ops, SparseCore 0:
  9.6 14.7 all-gather.4
  162.4 15.6 reduce-scatter.6
  193.4 13.2 all-gather.6
  247.3 15.6 reduce-scatter.8
  292.4 13.3 all-gather.8
  325.4 15.6 reduce-scatter.10
  357.6 13.2 all-gather.10
  553.8 12.0 reduce-scatter.12
  583.1 402.0 all-reduce.5
where the time goes:
time: 1010 us
  waiting for transfers between devices  531 us (53%)
  matrix products  194 us (19%)
  blocking collectives  98.2 us (10%)
  local copies, waits for them, and re-layouts  83.4 us (8%)
  other arithmetic  80.4 us (8%)
  between operations  14.9 us (1%)
    psum x1, waiting for transfers between devices, on_device(): lax.psum((grad_w_query, grad_b_query, grad_w_key, grad_w_value, grad_b_va...  309 us
    ppermute x2, waiting for transfers between devices, from_partner(): lax.ppermute(array, axis, [(i, i ^ 1 << distance) for i in range(lax.axis...  118 us
    psum x1, blocking collectives, on_device(): lax.psum((grad_w_query, grad_b_query, grad_w_key, grad_w_value, grad_b_va...  81.6 us
    dot_general x6, matrix products, product(): return jnp.dot(left, right, preferred_element_type=jnp.float32)  57 us
    unnamed x132, local copies, waits for them, and re-layouts  38 us
    dot_general x6, matrix products, back_product(): lax.dot_general(left, right, (((1,), (1,)), ((), ())), preferred_element_...  31.6 us
    dot_general x6, matrix products, weight_product(): lax.dot_general(left, right, (((0,), (0,)), ((), ())), preferred_element_...  25.9 us
  transfers between devices with their start and end apart: 11, of which 10 were waited for; matrix products, arithmetic and copies ran while one was open for 6% of the time, Pallas kernels for 0%

commit v1 on v0

v1 whole, which is shorter than its diff:
```python
import functools

import jax
import jax.numpy as jnp
from jax import lax
from jax.experimental import pallas as pl
from jax.experimental.pallas import tpu as pltpu
from jax.sharding import PartitionSpec as P

EPSILON = 1e-05
NEGATIVE = -1e30
ROOT_HALF = 0.7071067811865476
DENSITY_SCALE = 0.3989422804014327
F32 = jnp.float32
BF16 = jnp.bfloat16
MIB = 1 << 20


def dot(left, right, left_dim=1, right_dim=0):
    return lax.dot_general(
        left, right, (((left_dim,), (right_dim,)), ((), ())), preferred_element_type=F32
    )


def fill_bias(bias_ref, query_seg, keys_seg):
    same = keys_seg == query_seg
    covered = jnp.max(jnp.where(same, 1.0, 0.0), axis=0, keepdims=True)
    bias_ref[...] = jnp.where(same, 0.0, covered * NEGATIVE)


def attend_kernel(head_width, q_ref, k_ref, v_ref, qseg_ref, kseg_ref, ctx_ref, lse_ref, bias_ref):
    @pl.when(pl.program_id(1) == 0)
    def _():
        fill_bias(bias_ref, qseg_ref[0], kseg_ref[...])

    queries, keys = q_ref[...], k_ref[...]
    pair_width = queries.shape[1]
    value_cols = v_ref[...].astype(F32).T.astype(BF16)
    lane = lax.broadcasted_iota(jnp.int32, (1, pair_width), 1)
    parts, logs = [], []
    for low in range(0, pair_width, head_width):
        chosen = jnp.logical_and(lane >= low, lane < low + head_width)
        scores = dot(keys, jnp.where(chosen, queries, 0), 1, 1) + bias_ref[...]
        top = jnp.max(scores, axis=0, keepdims=True)
        shifted = jnp.exp(scores - top)
        total = jnp.sum(shifted, axis=0, keepdims=True)
        context = dot(value_cols[low : low + head_width], shifted.astype(BF16))
        parts.append(context * (1.0 / total))
        logs.append(top + jnp.log(total))
    ctx_ref[...] = jnp.concatenate(parts, axis=0).T.astype(BF16)
    lse_ref[0, 0] = jnp.concatenate(logs, axis=0)


def attend(queries, first_pair, keys, values, query_seg, keys_seg, head_width):
    seq_count, block_len = query_seg.shape
    pair = 2 * head_width
    pairs = keys.shape[1] // pair
    spec = pl.BlockSpec((block_len, pair), lambda s, p: (s, p))
    return pl.pallas_call(
        functools.partial(attend_kernel, head_width),
        grid=(seq_count, pairs),
        in_specs=[
            pl.BlockSpec((block_len, pair), lambda s, p: (s, p + first_pair)),
            spec,
            spec,
            pl.BlockSpec((1, 1, block_len), lambda s, p: (s, 0, 0)),
            pl.BlockSpec((block_len, 1), lambda s, p: (s, 0)),
        ],
        out_specs=[spec, pl.BlockSpec((1, 1, 2, block_len), lambda s, p: (s, p, 0, 0))],
        out_shape=[
            jax.ShapeDtypeStruct(keys.shape, BF16),
            jax.ShapeDtypeStruct((seq_count, pairs, 2, block_len), F32),
        ],
        scratch_shapes=[pltpu.VMEM((block_len, block_len), F32)],
        compiler_params=pltpu.CompilerParams(vmem_limit_bytes=48 * MIB),
        name="attend",
    )(queries, keys, values, query_seg[:, None, :], keys_seg.reshape(-1, 1))


def attend_back_kernel(
    head_width, scale, q_ref, k_ref, v_ref, g_ref, lse_ref, qseg_ref, kseg_ref,
    dq_ref, dk_ref, dv_ref, bias_ref,
):
    @pl.when(pl.program_id(1) == 0)
    def _():
        fill_bias(bias_ref, qseg_ref[0], kseg_ref[...])

    queries, keys, values, grads = q_ref[...], k_ref[...], v_ref[...], g_ref[...]
    pair_width = queries.shape[1]
    key_cols = keys.astype(F32).T.astype(BF16)
    lane = lax.broadcasted_iota(jnp.int32, (1, pair_width), 1)
    query_parts = []
    for at, low in enumerate(range(0, pair_width, head_width)):
        chosen = jnp.logical_and(lane >= low, lane < low + head_width)
        scores = dot(keys, jnp.where(chosen, queries, 0), 1, 1) + bias_ref[...]
        mixing = jnp.exp(scores - lse_ref[0, 0, at : at + 1, :])
        grad_mixing = dot(values, jnp.where(chosen, grads, 0), 1, 1)
        inner = jnp.sum(mixing * grad_mixing, axis=0, keepdims=True)
        grad_scores = (mixing * (grad_mixing - inner)).astype(BF16)
        grad_value = dot(mixing.astype(BF16), grads)
        grad_key = dot(grad_scores, queries)
        query_parts.append(dot(key_cols[low : low + head_width], grad_scores))
        if at == 0:
            all_value, all_key = grad_value, grad_key
        else:
            all_value = jnp.where(chosen, grad_value, all_value)
            all_key = jnp.where(chosen, grad_key, all_key)
    dq_ref[...] = (jnp.concatenate(query_parts, axis=0).T.astype(BF16) * scale).astype(BF16)
    dk_ref[...] = all_key.astype(BF16)
    dv_ref[...] = all_value.astype(BF16)


def attend_back(
    queries, first_pair, keys, values, grads, logs, query_seg, keys_seg, head_width, scale
):
    seq_count, block_len = query_seg.shape
    pair = 2 * head_width
    pairs = keys.shape[1] // pair
    spec = pl.BlockSpec((block_len, pair), lambda s, p: (s, p))
    return pl.pallas_call(
        functools.partial(attend_back_kernel, head_width, scale),
        grid=(seq_count, pairs),
        in_specs=[
            pl.BlockSpec((block_len, pair), lambda s, p: (s, p + first_pair)),
            spec,
            spec,
            pl.BlockSpec((block_len, pair), lambda s, p: (s, p + first_pair)),
            pl.BlockSpec((1, 1, 2, block_len), lambda s, p: (s, p, 0, 0)),
            pl.BlockSpec((1, 1, block_len), lambda s, p: (s, 0, 0)),
            pl.BlockSpec((block_len, 1), lambda s, p: (s, 0)),
        ],
        out_specs=[spec] * 3,
        out_shape=[jax.ShapeDtypeStruct(keys.shape, BF16)] * 3,
        scratch_shapes=[pltpu.VMEM((block_len, block_len), F32)],
        compiler_params=pltpu.CompilerParams(vmem_limit_bytes=48 * MIB),
        name="attend_back",
    )(queries, keys, values, grads, logs, query_seg[:, None, :], keys_seg.reshape(-1, 1))


def unit_rows(rows, width):
    mean = jnp.sum(rows, axis=1, keepdims=True) * (1.0 / width)
    centered = rows - mean
    variance = jnp.sum(centered * centered, axis=1, keepdims=True) * (1.0 / width)
    inverse = lax.rsqrt(variance + EPSILON)
    return centered * inverse, inverse


def unit_back(grad, unit, inverse, gain, width):
    scaled = grad * gain
    plain = jnp.sum(scaled, axis=1, keepdims=True) * (1.0 / width)
    along = jnp.sum(scaled * unit, axis=1, keepdims=True) * (1.0 / width)
    return (scaled - plain - unit * along) * inverse


def middle_kernel(
    chunk, ctxu_ref, ctxc_ref, x_ref, gout_ref, vec_ref, bup_ref, wo_ref,
    wup0_ref, wup1_ref, wdn0_ref, wdn1_ref,
    out_ref, act0_ref, act1_ref, gup0_ref, gup1_ref, normed_ref, gffn_ref, gattn_ref, gattnb_ref,
    gctx_ref, gvec_ref, gbup_ref, slope_ref,
):
    width = x_ref.shape[1]
    half = ctxu_ref.shape[1]
    part = wup0_ref.shape[1]

    @pl.when(pl.program_id(0) == 0)
    def _():
        gvec_ref[...] = jnp.zeros_like(gvec_ref)
        gbup_ref[...] = jnp.zeros_like(gbup_ref)

    def vec(i):
        return vec_ref[i : i + 1, :]

    def add_vec(i, rows):
        gvec_ref[i : i + 1, :] += jnp.sum(rows, axis=0, keepdims=True)

    attended = dot(ctxu_ref[...], wo_ref[:half]) + dot(ctxc_ref[...], wo_ref[half:])
    unit1, inverse1 = unit_rows(x_ref[...].astype(F32) + attended + vec(0), width)
    normed = unit1 * vec(1) + vec(2)
    normed_low = normed.astype(BF16)
    normed_ref[...] = normed_low
    pieces = ((wup0_ref, wdn0_ref, act0_ref, gup0_ref), (wup1_ref, wdn1_ref, act1_ref, gup1_ref))
    down = jnp.zeros_like(normed)
    for at, (wup, wdn, act_ref, _) in enumerate(pieces):
        for low in range(0, part, chunk):
            cols = slice(at * part + low, at * part + low + chunk)
            up = dot(normed_low, wup[:, low : low + chunk]) + bup_ref[:, cols]
            cumulative = 0.5 + 0.5 * lax.erf(up * ROOT_HALF)
            slope_ref[:, cols] = cumulative + up * (jnp.exp(-0.5 * up * up) * DENSITY_SCALE)
            activated = (up * cumulative).astype(BF16)
            act_ref[:, low : low + chunk] = activated
            down += dot(activated, wdn[low : low + chunk, :])
    unit2, inverse2 = unit_rows(normed + down + vec(3), width)
    out_ref[...] = unit2 * vec(4) + vec(5)
    grad_out = gout_ref[...]
    add_vec(4, grad_out * unit2)
    add_vec(5, grad_out)
    grad_ffn = unit_back(grad_out, unit2, inverse2, vec(4), width)
    add_vec(3, grad_ffn)
    grad_ffn_low = grad_ffn.astype(BF16)
    gffn_ref[...] = grad_ffn_low
    back = jnp.zeros_like(normed)
    for at, (wup, wdn, _, gup_ref) in enumerate(pieces):
        for low in range(0, part, chunk):
            cols = slice(at * part + low, at * part + low + chunk)
            grad_act = dot(grad_ffn_low, wdn[low : low + chunk, :], 1, 1)
            grad_up = (grad_act * slope_ref[:, cols]).astype(BF16)
            gup_ref[:, low : low + chunk] = grad_up
            gbup_ref[:, cols] += jnp.sum(grad_up.astype(F32), axis=0, keepdims=True)
            back += dot(grad_up, wup[:, low : low + chunk], 1, 1)
    grad_mid = grad_ffn + back
    add_vec(1, grad_mid * unit1)
    add_vec(2, grad_mid)
    grad_attn = unit_back(grad_mid, unit1, inverse1, vec(1), width)
    add_vec(0, grad_attn)
    gattn_ref[...] = grad_attn
    grad_attn_low = grad_attn.astype(BF16)
    gattnb_ref[...] = grad_attn_low
    gctx_ref[...] = dot(grad_attn_low, wo_ref[...], 1, 1).astype(BF16)


def middle(ctx_same, ctx_cross, x, grad_out, vectors, b_up, w_out, w_up, w_down):
    rows, width = x.shape
    half = ctx_same.shape[1]
    part = w_up[0].shape[1]
    tile = 256
    chunk = part // 2

    def tiles(cols):
        return pl.BlockSpec((tile, cols), lambda i: (i, 0))

    def whole(array):
        return pl.BlockSpec(array.shape, lambda i: (0, 0), pipeline_mode=pl.Buffered(1))

    def shape(cols, kind):
        return jax.ShapeDtypeStruct((rows, cols), kind)

    outs = [
        (width, F32), (part, BF16), (part, BF16), (part, BF16), (part, BF16),
        (width, BF16), (width, BF16), (width, F32), (width, BF16), (width, BF16),
    ]
    sums = [jax.ShapeDtypeStruct(vectors.shape, F32), jax.ShapeDtypeStruct(b_up.shape, F32)]
    weights = [vectors, b_up, w_out, *w_up, *w_down]
    return pl.pallas_call(
        functools.partial(middle_kernel, chunk),
        grid=(rows // tile,),
        in_specs=[tiles(half), tiles(half), tiles(width), tiles(width)] + [whole(w) for w in weights],
        out_specs=[tiles(c) for c, _ in outs]
        + [pl.BlockSpec(s.shape, lambda i: (0, 0)) for s in sums],
        out_shape=[shape(c, k) for c, k in outs] + sums,
        scratch_shapes=[pltpu.VMEM((tile, 2 * part), F32)],
        compiler_params=pltpu.CompilerParams(vmem_limit_bytes=60 * MIB),
        name="middle",
    )(ctx_same, ctx_cross, x, grad_out, *weights)


LINES = 4


class Item:
    def __init__(self, at, source, first, cols, order):
        self.at, self.source, self.first, self.cols, self.order = at, source, first, cols, order


def plan_items(count, cols):
    step = cols // 3
    orders = {1: "ABA", 2: "ABABAC", 3: "ABABACBAB"}[count]
    axes = {"A": ("x", "y", "z"), "B": ("y", "x", "z"), "C": ("z", "x", "y")}
    return [
        Item(i, i // 3, (i % 3) * step, step, axes[o]) for i, o in enumerate(orders)
    ]


def reduce_rows(order, rows):
    sizes = []
    for axis in order:
        rows = rows // (LINES if axis == "z" else 2)
        sizes.append(rows)
    return sizes


def sum_kernel(count, groups, items, *refs):
    own = refs[:count]
    other = refs[count : 2 * count]
    small_own, small_other = refs[2 * count : 2 * count + 2]
    refs = refs[2 * count + 2 :]
    out = refs[:count]
    small_out = refs[count]
    total, landing, small_land, send_sem, recv_sem, small_send, small_recv = (
        refs[count + 1 : count + 1 + count],
        refs[count + 1 + count : count + 1 + count + 5 * len(items)],
        *refs[count + 1 + count + 5 * len(items) :],
    )
    rows = own[0].shape[0]
    head, blk, dp = lax.axis_index("head"), lax.axis_index("blk"), lax.axis_index("dp")
    low, line, group = dp % 2, (dp // 2) % LINES, dp // (2 * LINES)
    partner = {
        "head": {"head": 1 - head},
        "x": {"blk": 1 - blk},
        "y": {"dp": dp + 1 - 2 * low},
    }
    line_partner = [
        {"dp": group * (2 * LINES) + ((line + d) % LINES) * 2 + low} for d in range(1, LINES)
    ]
    group_partner = [
        {"dp": ((group + d) % groups) * (2 * LINES) + line * 2 + low} for d in range(1, groups)
    ]
    everyone = [partner["head"], partner["x"], partner["y"]] + line_partner + group_partner
    barrier = pltpu.get_barrier_semaphore()
    for device in everyone:
        pl.semaphore_signal(barrier, inc=1, device_id=device, device_id_type=pl.DeviceIdType.MESH)
    pl.semaphore_wait(barrier, len(everyone))

    started = []

    def remote(source, target, sends, recvs, at, slot, device):
        copy = pltpu.make_async_remote_copy(
            src_ref=source,
            dst_ref=target,
            send_sem=sends.at[at, slot],
            recv_sem=recvs.at[at, slot],
            device_id=device,
            device_id_type=pl.DeviceIdType.MESH,
        )
        copy.start()
        started.append(copy)
        return copy

    z_slot, g_slot = 3, 3 + LINES - 1
    back_slot = g_slot + groups - 1

    def bufs(item):
        return landing[5 * item.at : 5 * item.at + 5]

    def cols(item):
        return slice(item.first, item.first + item.cols)

    def part(ref, start, size, item):
        return ref.at[pl.ds(pl.multiple_of(start, 16), size), cols(item)]

    def stages(item):
        hbuf, *bufs3, gbuf = bufs(item)
        mine = total[item.source]
        result = out[item.source]
        core = remote(
            other[item.source].at[:, cols(item)], hbuf, send_sem, recv_sem, item.at, 0,
            partner["head"],
        )
        yield
        core.wait_recv()
        mine[:, cols(item)] = (
            own[item.source][:, cols(item)].astype(F32) + hbuf[...].astype(F32)
        ).astype(BF16)
        start, size = 0, rows
        trail = []
        for buf, axis in zip(bufs3, item.order):
            trail.append((axis, start, size))
            if axis == "z":
                size = size // LINES
                copies = [
                    remote(
                        part(mine, start + ((line + d) % LINES) * size, size, item),
                        buf.at[d - 1], send_sem, recv_sem, item.at, z_slot + d - 1,
                        line_partner[d - 1],
                    )
                    for d in range(1, LINES)
                ]
                start = start + line * size
            else:
                size = size // 2
                bit = blk if axis == "x" else low
                copies = [
                    remote(
                        part(mine, start + (1 - bit) * size, size, item), buf.at[0],
                        send_sem, recv_sem, item.at, 1 if axis == "x" else 2, partner[axis],
                    )
                ]
                start = start + bit * size
            yield
            here = part(mine, start, size, item)
            value = here[...].astype(F32)
            for d, copy in enumerate(copies):
                copy.wait_recv()
                value = value + buf[d].astype(F32)
            here[...] = value.astype(BF16)
        if groups > 1:
            copies = [
                remote(
                    part(mine, start, size, item), gbuf.at[d - 1], send_sem, recv_sem, item.at,
                    g_slot + d - 1, group_partner[d - 1],
                )
                for d in range(1, groups)
            ]
            yield
            value = part(mine, start, size, item)[...].astype(F32)
            for d, copy in enumerate(copies):
                copy.wait_recv()
                value = value + gbuf[d].astype(F32)
            part(result, start, size, item)[...] = value.astype(BF16)
        else:
            part(result, start, size, item)[...] = part(mine, start, size, item)[...]
        for axis, before, whole in reversed(trail):
            here = part(result, start, size, item)
            if axis == "z":
                copies = [
                    remote(
                        here, here, send_sem, recv_sem, item.at, back_slot + 1 + d,
                        line_partner[d - 1],
                    )
                    for d in range(1, LINES)
                ]
            else:
                copies = [
                    remote(
                        here, here, send_sem, recv_sem, item.at,
                        back_slot + (0 if axis == "x" else 1), partner[axis],
                    )
                ]
            yield
            for copy in copies:
                copy.wait_recv()
            start, size = before, whole

    def small_stages():
        small_out[...] = small_own[...]
        copy = remote(
            small_other, small_land.at[0], small_send, small_recv, 0, 0, partner["head"]
        )
        yield
        copy.wait_recv()
        slot = 1
        value = small_own[...] + small_land[0]
        for devices in ([partner["x"]], [partner["y"]], line_partner, group_partner):
            if not devices:
                continue
            at = slot
            small_stage = small_land.at[slot]
            small_stage[...] = value
            slot += 1
            copies = []
            for device in devices:
                copies.append(
                    remote(
                        small_stage, small_land.at[slot], small_send, small_recv, 0, slot, device
                    )
                )
                slot += 1
            yield
            for d, copy in enumerate(copies):
                copy.wait_recv()
                value = value + small_land[at + 1 + d]
        small_out[...] = value

    running = [stages(item) for item in items] + [small_stages()]
    waiting = list(running)
    active = []
    while waiting or active:
        if waiting:
            active.append(waiting.pop(0))
        for stage in list(active):
            try:
                next(stage)
            except StopIteration:
                active.remove(stage)
    for copy in started:
        copy.wait_send()


def sum_gradients(own, other, small_own, small_other, dp_size, collective_id):
    count = len(own)
    rows, cols = own[0].shape
    groups = dp_size // (2 * LINES)
    items = plan_items(count, cols)
    landing = []
    for item in items:
        sizes = reduce_rows(item.order, rows)
        landing.append(pltpu.VMEM((rows, item.cols), BF16))
        for axis, size in zip(item.order, sizes):
            slots = LINES - 1 if axis == "z" else 1
            landing.append(pltpu.VMEM((slots, size, item.cols), BF16))
        landing.append(pltpu.VMEM((max(groups - 1, 1), sizes[-1], item.cols), BF16))
    slots = 3 + (LINES - 1) + (groups - 1) + 2 + (LINES - 1) + 1
    small_slots = 1 + 2 + 2 + LINES + groups
    vmem = pl.BlockSpec(memory_space=pltpu.VMEM)
    return pl.pallas_call(
        functools.partial(sum_kernel, count, groups, items),
        out_shape=[jax.ShapeDtypeStruct((rows, cols), BF16)] * count
        + [jax.ShapeDtypeStruct(small_own.shape, F32)],
        in_specs=[vmem] * count + [pl.BlockSpec(memory_space=pl.ANY)] * count + [vmem] * 2,
        out_specs=[vmem] * (count + 1),
        scratch_shapes=[pltpu.VMEM((rows, cols), BF16)] * count
        + landing
        + [
            pltpu.VMEM((small_slots, *small_own.shape), F32),
            pltpu.SemaphoreType.DMA((len(items), slots)),
            pltpu.SemaphoreType.DMA((len(items), slots)),
            pltpu.SemaphoreType.DMA((1, small_slots)),
            pltpu.SemaphoreType.DMA((1, small_slots)),
        ],
        compiler_params=pltpu.CompilerParams(
            collective_id=collective_id, has_side_effects=True, vmem_limit_bytes=60 * MIB
        ),
        name="sum_gradients",
    )(*own, *other, small_own, small_other)


def on_device(
    layer_in, segments, block_perm, w_query, b_query, w_key, w_value, b_value, w_attn_out,
    b_attn_out, norm1_gain, norm1_bias, w_up, b_up, w_down, b_down, norm2_gain, norm2_bias,
    grad_out,
):
    seq_count, block_len, half = layer_in.shape
    width = w_query.shape[0]
    local_heads = block_perm.shape[0]
    heads = 2 * local_heads
    head_cols = w_query.shape[1]
    head_width = head_cols // local_heads
    seqs = seq_count // 2
    rows = seqs * block_len
    scale = head_width ** (-0.5)
    head = lax.axis_index("head")
    my_block = lax.axis_index("blk")
    first = head == 0
    dp_size = lax.axis_size("dp")

    def swap(array):
        return lax.ppermute(array, "head", [(0, 1), (1, 0)])

    def cross(array):
        return lax.ppermute(array, "blk", [(0, 1), (1, 0)])

    def joined(mine, received, axis=-1):
        return jnp.where(
            first,
            jnp.concatenate([mine, received], axis=axis),
            jnp.concatenate([received, mine], axis=axis),
        )

    def to_tokens(array):
        mine = lax.dynamic_slice_in_dim(array, head * seqs, seqs, 0)
        theirs = lax.dynamic_slice_in_dim(array, (1 - head) * seqs, seqs, 0)
        return joined(mine, swap(theirs)).reshape(rows, width)

    def to_features(array):
        array = array.reshape(seqs, block_len, width)
        mine = lax.dynamic_slice_in_dim(array, head * half, half, 2)
        theirs = lax.dynamic_slice_in_dim(array, (1 - head) * half, half, 2)
        return joined(mine, swap(theirs), 0)

    x = to_tokens(layer_in)
    x_cross = jnp.concatenate(
        [cross(x[s * block_len : (s + 1) * block_len]) for s in range(seqs)]
    )
    model_vecs = [b_attn_out, norm1_gain, norm1_bias, b_down, norm2_gain, norm2_bias]
    packed = jnp.concatenate(
        [*model_vecs, b_query, b_value, b_up, block_perm.astype(F32).reshape(-1)]
    )
    packed_other = swap(packed)

    def unpack(array):
        vecs = array[: 8 * half].reshape(8, half)
        ups = array[8 * half : 8 * half + b_up.shape[0]]
        perm = array[8 * half + b_up.shape[0] :].reshape(block_perm.shape)
        return vecs, ups, perm

    vecs_own, up_own, perm_own = unpack(packed)
    vecs_other, up_other, perm_other = unpack(packed_other)
    vectors = joined(vecs_own, vecs_other)
    b_up_all = jnp.concatenate([up_own, up_other])[None, :]
    b_heads = jnp.concatenate([vecs_own[6:8], vecs_other[6:8]], axis=1)

    perm = jnp.concatenate([perm_own, perm_other], axis=0)
    columns = jnp.arange(perm.shape[1])
    reads = jnp.sum(jnp.where(columns[None, :] == my_block, perm, 0.0), axis=1)
    crossed = (reads != my_block.astype(F32)).astype(jnp.int32)
    before = jnp.cumsum(crossed) - crossed
    place = jnp.where(crossed == 1, heads // 2 + before, jnp.arange(heads) - before)
    feature = jnp.arange(heads * head_width)
    target = jnp.repeat(place, head_width) * head_width + feature % head_width
    sorter = (target[:, None] == feature[None, :]).astype(BF16)

    def sort_cols(own, other):
        return dot(jnp.concatenate([own, other], axis=1), sorter).astype(BF16)

    wq = sort_cols(w_query, swap(w_query))
    wk = sort_cols(w_key, swap(w_key))
    wv = sort_cols(w_value, swap(w_value))
    wo = dot(sorter, jnp.concatenate([w_attn_out, swap(w_attn_out)], axis=0), 0, 0).astype(BF16)
    b_sorted = jnp.sum(b_heads[:, :, None] * sorter.astype(F32)[None], axis=1)
    bq, bv = b_sorted[0], b_sorted[1]
    w_up_pair = (w_up, swap(w_up))
    w_down_pair = (w_down, swap(w_down))

    same = heads // 2 * head_width
    queries = ((dot(x, wq) + bq) * scale).astype(BF16)
    keys_same = dot(x, wk[:, :same]).astype(BF16)
    values_same = (dot(x, wv[:, :same]) + bv[:same]).astype(BF16)

    my_segments = lax.dynamic_slice_in_dim(segments, head * seqs, seqs, 0)
    own_seg = lax.dynamic_slice_in_dim(my_segments, my_block * block_len, block_len, 1)
    cross_seg = lax.dynamic_slice_in_dim(my_segments, (1 - my_block) * block_len, block_len, 1)
    ctx_same, log_same = attend(
        queries, 0, keys_same, values_same, own_seg, own_seg, head_width
    )
    keys_cross = dot(x_cross, wk[:, same:]).astype(BF16)
    values_cross = (dot(x_cross, wv[:, same:]) + bv[same:]).astype(BF16)
    pairs = same // (2 * head_width)
    ctx_cross, log_cross = attend(
        queries, pairs, keys_cross, values_cross, own_seg, cross_seg, head_width
    )

    grad_rows = to_tokens(grad_out)
    (
        out_rows, act0, act1, gup0, gup1, normed, grad_ffn, grad_attn, grad_attn_low, grad_ctx,
        grad_vecs, grad_bup,
    ) = middle(
        ctx_same, ctx_cross, x, grad_rows, vectors, b_up_all, wo, w_up_pair, w_down_pair
    )
    layer_out = to_features(out_rows)

    def weight(left, right):
        return dot(left, right, 0, 0).astype(BF16)

    def down_grad(act):
        middle_col = act.shape[1] // 2
        return jnp.concatenate(
            [weight(act[:, :middle_col], grad_ffn), weight(act[:, middle_col:], grad_ffn)], axis=1
        )

    gup_own, gup_other = weight(normed, gup0), weight(normed, gup1)
    gdn_own, gdn_other = down_grad(act0), down_grad(act1)

    dq_cross, dk_cross, dv_cross = attend_back(
        queries, pairs, keys_cross, values_cross, grad_ctx, log_cross, own_seg, cross_seg,
        head_width, scale,
    )
    back_cross = (dot(dk_cross, wk[:, same:], 1, 1) + dot(dv_cross, wv[:, same:], 1, 1)).astype(
        BF16
    )
    returned = cross(back_cross)
    dq_same, dk_same, dv_same = attend_back(
        queries, 0, keys_same, values_same, grad_ctx, log_same, own_seg, own_seg, head_width, scale
    )

    grad_sorted = jnp.concatenate(
        [
            jnp.concatenate([weight(x, dq_same), weight(x, dq_cross)], axis=1),
            jnp.concatenate([weight(x, dk_same), weight(x_cross, dk_cross)], axis=1),
            jnp.concatenate([weight(x, dv_same), weight(x_cross, dv_cross)], axis=1),
        ],
        axis=0,
    )
    grad_natural = dot(grad_sorted, sorter, 1, 1).astype(BF16).reshape(3, width, 2, head_cols)
    grad_wo = jnp.concatenate(
        [weight(ctx_same, grad_attn_low), weight(ctx_cross, grad_attn_low)], axis=0
    )
    grad_wo = dot(sorter, grad_wo).astype(BF16).reshape(2, head_cols, 2, width // 2)

    def heads_part(at):
        out_rows_part = grad_wo[at].transpose(1, 0, 2).reshape(2 * head_cols, width // 2)
        return jnp.concatenate([*(grad_natural[i, :, at] for i in range(3)), out_rows_part], axis=1)

    dq = jnp.concatenate([dq_same, dq_cross], axis=1).astype(F32)
    dv = jnp.concatenate([dv_same, dv_cross], axis=1).astype(F32)
    grad_bq = jnp.sum(sorter.astype(F32) * jnp.sum(dq, axis=0)[None, :], axis=1)
    grad_bv = jnp.sum(sorter.astype(F32) * jnp.sum(dv, axis=0)[None, :], axis=1)
    up_cols = b_up.shape[0]

    def small_part(at, mine):
        vec_part = lax.dynamic_slice_in_dim(
            grad_vecs[:6], (head if mine else 1 - head) * half, half, 1
        )
        flat = jnp.concatenate(
            [
                vec_part.reshape(-1),
                grad_bq[at * head_cols : (at + 1) * head_cols],
                grad_bv[at * head_cols : (at + 1) * head_cols],
                grad_bup[0, at * up_cols : (at + 1) * up_cols],
            ]
        )
        return jnp.pad(flat, (0, 8 * up_cols - flat.shape[0])).reshape(8, up_cols)

    total_up, total_down, total_heads, small = sum_gradients(
        [gup_own, gdn_own, heads_part(0)],
        [gup_other, gdn_other, heads_part(1)],
        small_part(0, True),
        small_part(1, False),
        dp_size,
        1,
    )
    grad_in_rows = (
        grad_attn
        + dot(dq_same, wq[:, :same], 1, 1)
        + dot(dq_cross, wq[:, same:], 1, 1)
        + dot(dk_same, wk[:, :same], 1, 1)
        + dot(dv_same, wv[:, :same], 1, 1)
        + returned.astype(F32)
    )
    grad_in = to_features(grad_in_rows)

    small = small.reshape(-1)
    vec_totals = small[: 8 * half].reshape(8, half)
    heads_total = total_heads.astype(F32)
    down_total = total_down.astype(F32)
    out_total = heads_total[:, 3 * head_cols :]
    grad_w_attn_out = jnp.concatenate([out_total[:head_cols], out_total[head_cols:]], axis=1)
    grad_w_down = jnp.concatenate([down_total[:, :width], down_total[:, width:]], axis=0)
    return (
        layer_out,
        grad_in,
        heads_total[:, :head_cols],
        vec_totals[6],
        heads_total[:, head_cols : 2 * head_cols],
        heads_total[:, 2 * head_cols : 3 * head_cols],
        vec_totals[7],
        grad_w_attn_out,
        vec_totals[0],
        vec_totals[1],
        vec_totals[2],
        total_up.astype(F32),
        small[8 * half : 8 * half + up_cols],
        grad_w_down,
        vec_totals[3],
        vec_totals[4],
        vec_totals[5],
    )


def solution(mesh):
    rows, cols, vec = P("head", None), P(None, "head"), P("head")
    tokens = P("dp", "blk", "head")
    return jax.shard_map(
        on_device,
        mesh=mesh,
        in_specs=(
            tokens, P("dp", None), rows, cols, vec, cols, cols, vec, rows, vec, vec, vec, cols,
            vec, rows, vec, vec, vec, tokens,
        ),
        out_specs=(
            tokens, tokens, cols, vec, cols, cols, vec, rows, vec, vec, vec, cols, vec, rows, vec,
            vec, vec,
        ),
        check_vma=False,
    )
```

time: 1010 us -> 490 us (0.49)
  waiting for transfers between devices: 531 us -> 22.2 us
  Pallas kernels: 0 us -> 285 us
  matrix products: 194 us -> 84 us
  blocking collectives: 98.2 us -> 0 us
  other arithmetic: 80.4 us -> 29.1 us
  local copies, waits for them, and re-layouts: 83.4 us -> 54.2 us
  between operations: 14.9 us -> 1.97 us
    psum x1 -> x0, waiting for transfers between devices: 309 us -> none  [on_device(): lax.psum((grad_w_query, grad_b_query, grad_w_key, grad_w_value, grad_b_va...]
    pallas_call x0 -> x6, Pallas kernels: none -> 285 us  [the longest x1 192 us: sum_gradients(): pl.pallas_call(functools.partial(sum_kernel, count, groups, items), out_s...]
    dot_general x46 -> x31, matrix products: 194 us -> 84 us  [dot(): lax.dot_general(left, right, (((left_dim,), (right_dim,)), ((), ())), pre...]
    psum x7 -> x0, blocking collectives: 98.2 us -> none  [the longest x1 81.6 us: on_device(): lax.psum((grad_w_query, grad_b_query, grad_w_key, grad_w_value, grad_b_va...]
    ppermute x2 -> x14, waiting for transfers between devices: 118 us -> 22.2 us  [the longest x3 22.2 us: cross(): return lax.ppermute(array, 'blk', [(0, 1), (1, 0)])]
    all_gather x4 -> x0, waiting for transfers between devices: 56.5 us -> none  [the longest x1 16.4 us: on_device(): full_in = lax.all_gather(layer_in, 'head', axis=2, tiled=True)]
    reduce_scatter x3 -> x0, waiting for transfers between devices: 47.4 us -> none  [the longest x1 15.8 us: on_device(): lax.psum_scatter(attn_part, 'head', scatter_dimension=2, tiled=True)]
    reduce_sum x17 -> x4, other arithmetic: 45.4 us -> 1.75 us  [the longest x1 0.75 us: on_device(): grad_bq = jnp.sum(sorter.astype(F32) * jnp.sum(dq, axis=0)[None, :], axis=1)]
  transfers between devices with their start and end apart: 11 -> 14, of which waited for: 10 -> 1; matrix products, arithmetic and copies ran while one was open for 6% -> 17% of each run, Pallas kernels for 0% -> 44%
where the time goes in v1:
time: 490 us; the launch traced here: 483 us
  Pallas kernels  285 us (58%)
  matrix products  84 us (17%)
  local copies, waits for them, and re-layouts  54.2 us (11%)
  other arithmetic  29.1 us (6%)
  waiting for transfers between devices  22.2 us (5%)
  starting transfers between devices  6.7 us (1%)
    pallas_call x1, Pallas kernels, sum_gradients(): pl.pallas_call(functools.partial(sum_kernel, count, groups, items), out_s...  192 us
    dot_general x31, matrix products, dot(): lax.dot_general(left, right, (((left_dim,), (right_dim,)), ((), ())), pre...  84 us
    pallas_call x1, Pallas kernels, middle(): pl.pallas_call(functools.partial(middle_kernel, chunk), grid=(rows // til...  38.4 us
    pallas_call x2, Pallas kernels, attend_back(): pl.pallas_call(functools.partial(attend_back_kernel, head_width, scale),...  36.1 us
    ppermute x3, waiting for transfers between devices, cross(): return lax.ppermute(array, 'blk', [(0, 1), (1, 0)])  22.2 us
    pallas_call x2, Pallas kernels, attend(): pl.pallas_call(functools.partial(attend_kernel, head_width), grid=(seq_co...  18.3 us
    unnamed x152, local copies, waits for them, and re-layouts  16.5 us
    select_n x6, other arithmetic, joined(): jnp.where(first, jnp.concatenate([mine, received], axis=axis), jnp.concat...  11.2 us
  transfers between devices with their start and end apart: 14, of which 1 were waited for; matrix products, arithmetic and copies ran while one was open for 17% of the time, Pallas kernels for 44%

profile of v1, /device:TPU:0, one launch (start us, length us, event | category | flops | bytes accessed | tf_op | source)
XLA Modules:
  0.0 483.2 jit_solution(8249008994183199049)
XLA Ops:
  10.0 2.6 constant_dynamic-slice_fusion.9
  18.3 2.5 fusion.37
  21.0 2.8 fusion.38
  23.9 2.8 fusion.39
  26.7 3.8 fusion.40.wo_ref
  38.5 9.2 %attend.2 = (bf16[1024,384]{1,0:T(8,128)(2,1)S(1)}, f32[2,3,2,512]{3,2,1,0:T(2,128)S(1)}) custom-call(bf16[1024,768]{1,0:T(8,128)(2,1)S(1)} %multiply_convert_fusion.q_ref, bf16[1024,384]{1,0:T(8,128)(2,1)S(1)} %convolution_convert_fusion.4.k_ref, bf16[1024,384]{1,0:T(8,128)(2,1)S(1)} %add_convert_fusion.2.v_ref, ...), custom_call_target="tpu_custom_call" | custom-call | tf_op jit(solution)/shard_map/attend/pallas_call | solution.py:59
  47.8 22.2 %collective-permute-done.5 = bf16[512,768]{1,0:T(8,128)(2,1)} collective-permute-done((bf16[512,768]{1,0:T(8,128)(2,1)}, bf16[512,768]{1,0:T(8,128)(2,1)}, u32[]{:S(2)}, u32[]{:S(2)}) %collective-permute-start.5) | collective-permute-done | bytes 786464 | tf_op jit(solution)/shard_map/ppermute | solution.py:529
  74.6 9.1 %attend.3 = (bf16[1024,384]{1,0:T(8,128)(2,1)S(1)}, f32[2,3,2,512]{3,2,1,0:T(2,128)S(1)}) custom-call(bf16[1024,768]{1,0:T(8,128)(2,1)S(1)} %multiply_convert_fusion.q_ref, bf16[1024,384]{1,0:T(8,128)(2,1)S(1)} %convolution_convert_fusion.3.k_ref, bf16[1024,384]{1,0:T(8,128)(2,1)S(1)} %add_convert_fusion.1.v_ref, ...), custom_call_target="tpu_custom_call" | custom-call | tf_op jit(solution)/shard_map/attend/pallas_call | solution.py:59
  83.7 4.1 maximum_select_fusion.gout_ref
  89.3 38.4 %middle.1 = (f32[1024,768]{1,0:T(8,128)}, bf16[1024,1536]{1,0:T(8,128)(2,1)}, bf16[1024,1536]{1,0:T(8,128)(2,1)}, bf16[1024,1536]{1,0:T(8,128)(2,1)}, bf16[1024,...) custom-call(bf16[1024,384]{1,0:T(8,128)(2,1)} %copy-done, ...), custom_call_target="tpu_custom_call" | custom-call | tf_op jit(solution)/shard_map/middle/pallas_call | solution.py:243
  130.9 13.7 %attend_back.3 = (bf16[1024,384]{1,0:T(8,128)(2,1)S(1)}, bf16[1024,384]{1,0:T(8,128)(2,1)S(1)}, bf16[1024,384]{1,0:T(8,128)(2,1)S(1)}) custom-call(bf16[1024,768]{1,0:T(8,128)(2,1)S(1)} %multiply_convert_fusion.q_ref, bf16[1024,384]{1,0:T(8,128)(2,1)S(1)} %copy-done.11, bf16[1024,384]{1,0:T(8,128)(2,1)S(1)} %copy-done.13, ...), custom_call_target="tpu_custom_call" | custom-call | tf_op jit(solution)/shard_map/attend_back/pallas_call | solution.py:120
  145.6 22.4 %attend_back.2 = (bf16[1024,384]{1,0:T(8,128)(2,1)S(1)}, bf16[1024,384]{1,0:T(8,128)(2,1)S(1)}, bf16[1024,384]{1,0:T(8,128)(2,1)S(1)}) custom-call(bf16[1024,768]{1,0:T(8,128)(2,1)S(1)} %multiply_convert_fusion.q_ref, bf16[1024,384]{1,0:T(8,128)(2,1)S(1)} %copy-done.9, bf16[1024,384]{1,0:T(8,128)(2,1)S(1)} %copy-done.7, ...), custom_call_target="tpu_custom_call" | custom-call | tf_op jit(solution)/shard_map/attend_back/pallas_call | solution.py:120
  186.6 2.7 fusion.68
  192.6 3.9 constant_dynamic-slice_fusion.5
  202.6 21.5 %convolution_convert_fusion = bf16[2304,768]{1,0:T(8,128)(2,1)} fusion(bf16[768,384]{0,1:T(8,128)(2,1)S(1)} %copy-done.65, bf16[768,384]{0,1:T(8,128)(2,1)S(1)} %copy-done.68, bf16[768,384]{0,1:T(8,128)(2,1)S(1)} %convolution_convert_fusion.9, bf16[768,384]{0,1:T(8,128)(2,1)S(1)} %convolution_convert_fusion.10, bf16[768,384]{0,1:T(8,128)(2,1)S(1)} %copy-done.66, ...), kind=kOutput, calls=%fused_computation | convolution fusion | flops 2741501952 | bytes 7080960 | tf_op jit(solution)/shard_map/dot_general | solution.py:20
  224.1 8.1 %reshape.212 = bf16[3,768,2,384]{3,2,1,0:T(2,128)(2,1)} reshape(bf16[2304,768]{1,0:T(8,128)(2,1)} %convolution_convert_fusion) | data formatting | bytes 7077888 | tf_op jit(solution)/shard_map/reshape | solution.py:652
  232.3 4.4 add_convert_fusion
  238.5 4.0 convolution_convert_fusion.2.refs_0_
  242.4 4.0 convolution_convert_fusion.1.refs_3_
  246.4 4.9 %fusion.94 = (bf16[1,768,1,384]{3,2,1,0:T(2,128)(2,1)S(1)}, bf16[1,768,1,384]{3,2,1,0:T(2,128)(2,1)S(1)}, bf16[1,768,1,384]{3,2,1,0:T(2,128)(2,1)S(1)}, bf16[1,7...) fusion(bf16[3,768,2,384]{3,2,1,0:T(2,128)(2,1)S(1)} %copy-done.19), kind=kLoop, calls=%fused_computation.190 | loop fusion | bytes 7077888 | tf_op jit(solution)/shard_map/slice | solution.py:660
  259.5 192.1 %sum_gradients.1 = (bf16[768,1536]{1,0:T(8,128)(2,1)}, bf16[768,1536]{1,0:T(8,128)(2,1)}, bf16[768,1536]{1,0:T(8,128)(2,1)}, f32[8,1536]{1,0:T(8,128)}) custom-call(bf16[768,1536]{1,0:T(8,128)(2,1)} %convolution_convert_fusion.2.refs_0_, bf16[768,1536]{1,0:T(8,128)(2,1)} %get-tuple-element.140.refs_1_, bf16[768,1536]{1,0:T(8,128)(2,1)} %pad_maximum_fusion.2.refs_2_, ...), custom_call_target="tpu_custom_call" | custom-call | tf_op jit(solution)/shard_map/sum_gradients/pallas_call | solution.py:484
  458.7 2.9 convert_add_fusion
  465.1 4.6 convert_element_type.173
  477.2 3.9 maximum_select_fusion.1
  (271 shorter events, 90.7 us)
Async XLA Ops:
  7.8 7.3 %collective-permute-start.2 = (f32[4620]{0:T(1024)S(1)}, f32[4620]{0:T(1024)S(1)}, u32[]{:S(2)}, u32[]{:S(2)}) collective-permute-start(f32[4620]{0:T(1024)S(1)} %constant_dynamic-update-slice_fusion.19), channel_id=1, source_target_pairs={{0,16},{16,0},{1,17},{17,1},{2,18},{18,2},{3,19},{19,3},{4,20},{20... | collective-permute-start | bytes 55448 | tf_op jit(solution)/shard_map/ppermute | solution.py:526
  8.3 9.5 %collective-permute-start.1 = (bf16[768,384]{1,0:T(8,128)(2,1)}, bf16[768,384]{1,0:T(8,128)(2,1)}, u32[]{:S(2)}, u32[]{:S(2)}) collective-permute-start(bf16[768,384]{1,0:T(8,128)(2,1)} %param.22), channel_id=1, source_target_pairs={{0,16},{16,0},{1,17},{17,1},{2,18},{18,2},{3,19},{19,3},{4,20},{20... | collective-permute-start | bytes 1769480 | tf_op jit(solution)/shard_map/ppermute | solution.py:526
  8.4 12.5 %collective-permute-start.3 = (bf16[768,384]{1,0:T(8,128)(2,1)}, bf16[768,384]{1,0:T(8,128)(2,1)}, u32[]{:S(2)}, u32[]{:S(2)}) collective-permute-start(bf16[768,384]{1,0:T(8,128)(2,1)} %param.24), channel_id=1, source_target_pairs={{0,16},{16,0},{1,17},{17,1},{2,18},{18,2},{3,19},{19,3},{4,20},{20... | collective-permute-start | bytes 1769480 | tf_op jit(solution)/shard_map/ppermute | solution.py:526
  8.8 15.0 %collective-permute-start.4 = (bf16[768,384]{1,0:T(8,128)(2,1)}, bf16[768,384]{1,0:T(8,128)(2,1)}, u32[]{:S(2)}, u32[]{:S(2)}) collective-permute-start(bf16[768,384]{1,0:T(8,128)(2,1)} %param.25), channel_id=1, source_target_pairs={{0,16},{16,0},{1,17},{17,1},{2,18},{18,2},{3,19},{19,3},{4,20},{20... | collective-permute-start | bytes 1769480 | tf_op jit(solution)/shard_map/ppermute | solution.py:526
  8.9 17.9 %collective-permute-start.8 = (bf16[384,768]{1,0:T(8,128)(2,1)}, bf16[384,768]{1,0:T(8,128)(2,1)}, u32[]{:S(2)}, u32[]{:S(2)}) collective-permute-start(bf16[384,768]{1,0:T(8,128)(2,1)} %param.27), channel_id=1, source_target_pairs={{0,16},{16,0},{1,17},{17,1},{2,18},{18,2},{3,19},{19,3},{4,20},{20... | collective-permute-start | bytes 1769480 | tf_op jit(solution)/shard_map/ppermute | solution.py:526
  15.1 15.5 %collective-permute-start = (bf16[2,512,384]{2,1,0:T(8,128)(2,1)}, bf16[2,512,384]{2,1,0:T(8,128)(2,1)S(1)}, u32[]{:S(2)}, u32[]{:S(2)}) collective-permute-start(bf16[2,512,384]{2,1,0:T(8,128)(2,1)} %get-tuple-element.105), channel_id=1, source_target_pairs={{0,16},{16,0},{1,17},{17,1},{2,18},{18,2},{3,19},{19,3},{4,20},{20... | collective-permute-start | bytes 2359304 | tf_op jit(solution)/shard_map/ppermute | solution.py:526
  17.8 70.0 %collective-permute-start.9 = (bf16[768,1536]{1,0:T(8,128)(2,1)S(1)}, bf16[768,1536]{1,0:T(8,128)(2,1)S(1)}, u32[]{:S(2)}, u32[]{:S(2)}) collective-permute-start(bf16[768,1536]{1,0:T(8,128)(2,1)S(1)} %copy-done.30), channel_id=1, source_target_pairs={{0,16},{16,0},{1,17},{17,1},{2,18},{18,2},{3,19},{19,3},{4,20},{20... | collective-permute-start | bytes 7077896 | tf_op jit(solution)/shard_map/ppermute | solution.py:526
  20.9 16.2 %copy-start.36 = (bf16[768,768]{1,0:T(8,128)(2,1)}, bf16[768,768]{1,0:T(8,128)(2,1)S(1)}, u32[]{:S(2)}) copy-start(bf16[768,768]{1,0:T(8,128)(2,1)S(1)} %fusion.37) | copy-start | bytes 3538948
  20.9 66.9 %collective-permute-start.10 = (bf16[1536,768]{1,0:T(8,128)(2,1)S(1)}, bf16[1536,768]{1,0:T(8,128)(2,1)}, u32[]{:S(2)}, u32[]{:S(2)}) collective-permute-start(bf16[1536,768]{1,0:T(8,128)(2,1)S(1)} %copy-done.31), channel_id=1, source_target_pairs={{0,16},{16,0},{1,17},{17,1},{2,18},{18,2},{3,19},{19,3},{4,20},{20... | collective-permute-start | bytes 7077896 | tf_op jit(solution)/shard_map/ppermute | solution.py:526
  23.8 12.3 %copy-start.38 = (bf16[768,768]{1,0:T(8,128)(2,1)}, bf16[768,768]{1,0:T(8,128)(2,1)S(1)}, u32[]{:S(2)}) copy-start(bf16[768,768]{1,0:T(8,128)(2,1)S(1)} %fusion.38) | copy-start | bytes 3538948
  23.8 59.9 %collective-permute-start.7 = (f32[2,512,384]{2,1,0:T(8,128)}, f32[2,512,384]{2,1,0:T(8,128)}, u32[]{:S(2)}, u32[]{:S(2)}) collective-permute-start(f32[2,512,384]{2,1,0:T(8,128)} %get-tuple-element.94), channel_id=1, source_target_pairs={{0,16},{16,0},{1,17},{17,1},{2,18},{18,2},{3,19},{19,3},{4,20},{20... | collective-permute-start | bytes 4718600 | tf_op jit(solution)/shard_map/ppermute | solution.py:526
  32.2 39.1 %collective-permute-start.6 = (bf16[512,768]{1,0:T(8,128)(2,1)}, bf16[512,768]{1,0:T(8,128)(2,1)}, u32[]{:S(2)}, u32[]{:S(2)}) collective-permute-start(bf16[512,768]{1,0:T(8,128)(2,1)} %get-tuple-element.102), channel_id=1, source_target_pairs={{0,8},{8,0},{1,9},{9,1},{2,10},{10,2},{3,11},{11,3},{4,12},{12,4},... | collective-permute-start | bytes 2359304 | tf_op jit(solution)/shard_map/ppermute | solution.py:529
  34.7 35.3 %collective-permute-start.5 = (bf16[512,768]{1,0:T(8,128)(2,1)}, bf16[512,768]{1,0:T(8,128)(2,1)}, u32[]{:S(2)}, u32[]{:S(2)}) collective-permute-start(bf16[512,768]{1,0:T(8,128)(2,1)} %get-tuple-element.103), channel_id=1, source_target_pairs={{0,8},{8,0},{1,9},{9,1},{2,10},{10,2},{3,11},{11,3},{4,12},{12,4},... | collective-permute-start | bytes 2359304 | tf_op jit(solution)/shard_map/ppermute | solution.py:529
  47.8 25.7 %copy-start = (bf16[1024,384]{1,0:T(8,128)(2,1)}, bf16[1024,384]{1,0:T(8,128)(2,1)S(1)}, u32[]{:S(2)}) copy-start(bf16[1024,384]{1,0:T(8,128)(2,1)S(1)} %get-tuple-element.43.ctxu_ref) | copy-start | bytes 2359300
  47.8 24.7 %copy-start.39 = (bf16[768,768]{1,0:T(8,128)(2,1)S(1)}, bf16[768,768]{1,0:T(8,128)(2,1)}, u32[]{:S(2)}) copy-start(bf16[768,768]{1,0:T(8,128)(2,1)} %copy-done.38) | copy-start | bytes 3538948
  73.5 10.1 %copy-start.10 = (bf16[1024,384]{1,0:T(8,128)(2,1)}, bf16[1024,384]{1,0:T(8,128)(2,1)S(1)}, u32[]{:S(2)}) copy-start(bf16[1024,384]{1,0:T(8,128)(2,1)S(1)} %convolution_convert_fusion.3.k_ref) | copy-start | bytes 2359300
  74.6 13.3 %copy-start.12 = (bf16[1024,384]{1,0:T(8,128)(2,1)}, bf16[1024,384]{1,0:T(8,128)(2,1)S(1)}, u32[]{:S(2)}) copy-start(bf16[1024,384]{1,0:T(8,128)(2,1)S(1)} %add_convert_fusion.1.v_ref) | copy-start | bytes 2359300
  89.3 38.4 %copy-start.3 = (bf16[1024,384]{1,0:T(8,128)(2,1)S(1)}, bf16[1024,384]{1,0:T(8,128)(2,1)}, u32[]{:S(2)}) copy-start(bf16[1024,384]{1,0:T(8,128)(2,1)} %copy-done.2) | copy-start | bytes 2359300
  130.9 14.6 %copy-start.7 = (bf16[1024,384]{1,0:T(8,128)(2,1)S(1)}, bf16[1024,384]{1,0:T(8,128)(2,1)}, u32[]{:S(2)}) copy-start(bf16[1024,384]{1,0:T(8,128)(2,1)} %copy-done.6) | copy-start | bytes 2359300
  130.9 14.6 %copy-start.9 = (bf16[1024,384]{1,0:T(8,128)(2,1)S(1)}, bf16[1024,384]{1,0:T(8,128)(2,1)}, u32[]{:S(2)}) copy-start(bf16[1024,384]{1,0:T(8,128)(2,1)} %copy-done.8) | copy-start | bytes 2359300
  145.5 22.5 %copy-start.50 = (bf16[1024,768]{1,0:T(8,128)(2,1)S(1)}, bf16[1024,768]{1,0:T(8,128)(2,1)}, u32[]{:S(2)}) copy-start(bf16[1024,768]{1,0:T(8,128)(2,1)} %copy-done.49) | copy-start | bytes 4718596
  232.2 245.0 %collective-permute-start.11 = (f32[2,512,384]{2,1,0:T(8,128)}, f32[2,512,384]{2,1,0:T(8,128)}, u32[]{:S(2)}, u32[]{:S(2)}) collective-permute-start(f32[2,512,384]{2,1,0:T(8,128)} %get-tuple-element.92), channel_id=1, source_target_pairs={{0,16},{16,0},{1,17},{17,1},{2,18},{18,2},{3,19},{19,3},{4,20},{20... | collective-permute-start | bytes 4718600 | tf_op jit(solution)/shard_map/ppermute | solution.py:526
  236.7 220.7 %collective-permute-start.12 = (bf16[1024,768]{1,0:T(8,128)(2,1)}, bf16[1024,768]{1,0:T(8,128)(2,1)}, u32[]{:S(2)}, u32[]{:S(2)}) collective-permute-start(bf16[1024,768]{1,0:T(8,128)(2,1)} %add_convert_fusion), channel_id=1, source_target_pairs={{0,8},{8,0},{1,9},{9,1},{2,10},{10,2},{3,11},{11,3},{4,12},{12,4},... | collective-permute-start | bytes 4718600 | tf_op jit(solution)/shard_map/ppermute | solution.py:529
  462.9 18.3 %collective-permute-start.13 = (f32[2,512,384]{2,1,0:T(8,128)}, f32[2,512,384]{2,1,0:T(8,128)S(1)}, u32[]{:S(2)}, u32[]{:S(2)}) collective-permute-start(f32[2,512,384]{2,1,0:T(8,128)} %get-tuple-element.90), channel_id=1, source_target_pairs={{0,16},{16,0},{1,17},{17,1},{2,18},{18,2},{3,19},{19,3},{4,20},{20... | collective-permute-start | bytes 4718600 | tf_op jit(solution)/shard_map/ppermute | solution.py:526
  (59 other events, 167.5 us)
